TPU v7x, 32 devices: a whole 2x2x4 slice. The times are simulated.
32 devices in a mesh: dom: 16 (over z, y, x), sub: 2 (over core).
Axes of the slice: x: 2, y: 2, z: 4, core: 2. Of those that a mesh axis runs over, the one named last changes fastest.
Arguments:
- a_blocks: bfloat16 [2048, 8, 128, 128], P(('dom', 'sub')), may hold values from -6 to 6
- nbr_offset: int32 [2048, 8], P(('dom', 'sub')), may hold values from -3 to 3
- nbr_count: int32 [2048], P(('dom', 'sub')), may hold values from 4 to 8
- prolong: bfloat16 [2048, 128, 128], P(('dom', 'sub')), may hold values from -0.5 to 0.5
- owner_start: int32 [32], replicated, may hold values from 0 to 2047, as said below
Outputs:
- coarse: float32 [512, 7, 128, 128], P(('dom', 'sub'))
Inputs may be any that keep to these rules, and one draw needn't show every extreme that they name: owner_start[0] = 0, owner_start[1] = 112, and owner_start[d] - d * 64 lies in 0 to 48 for every d.
All inputs are finite; a program needn't handle non-finite values.
Results may differ from a plain program's by a relative error of at most 0.0029.
Values may be sent and summed in bfloat16 or wider, within the bound.
No kernel may reach another device: no remote copies, remote signals or barrier semaphores. Data moves between devices by JAX's collectives and lax.ppermute only.
A program may use at most 256 MiB of HBM per device.

v0:
```python
import jax
import jax.numpy as jnp
from jax import lax
from jax.sharding import PartitionSpec as P

W = 3
KC = 7
AD = 16


def with_halo(x, sides, width):
    for axis, dim in sides:
        count, length = (lax.axis_size(axis), x.shape[dim])
        up = [(i, (i + 1) % count) for i in range(count - 1)]
        down = [(j, i) for i, j in up]
        last = lax.slice_in_dim(x, length - width, length, axis=dim)
        initial = lax.slice_in_dim(x, 0, width, axis=dim)
        before = lax.ppermute(last, axis, up)
        after = lax.ppermute(initial, axis, down)
        x = jnp.concatenate([before, x, after], axis=dim)
    return x


def passed_along(block, axis, distance):
    devices = range(lax.axis_size(axis))
    route = [(i - distance, i) for i in devices if i - distance in devices]
    return lax.ppermute(block, axis, route)


def aggregate_ids(fine_ids, owner_start, total_rows):
    flat_ids = fine_ids.reshape(-1)
    bounds = jnp.concatenate([owner_start, jnp.full((1,), total_rows, jnp.int32)])
    owner_index = jnp.sum((owner_start[None, :] <= flat_ids[:, None]).astype(jnp.int32), axis=1) - 1
    first_row = bounds[owner_index]
    span_rows = bounds[owner_index + 1] - first_row
    local_ids = (flat_ids - first_row) * AD // span_rows
    return (owner_index * AD + local_ids).reshape(fine_ids.shape)


def galerkin_rows(blocks, window, offsets, counts, fine_ids, owner_start, total_rows):
    count_rows = blocks.shape[0]
    slots_row = blocks.shape[1]
    local_index = jnp.arange(count_rows, dtype=jnp.int32)[:, None] + W + offsets
    near_rows = window[local_index]
    products = jnp.einsum("rkab,rkbc->rkac", blocks, near_rows, preferred_element_type=jnp.float32)
    neighbour = fine_ids[:, None] + offsets
    is_valid = (
        (jnp.arange(slots_row, dtype=jnp.int32)[None, :] < counts[:, None])
        & (neighbour >= 0)
        & (neighbour < total_rows)
    )
    row_aggs = aggregate_ids(jnp.clip(fine_ids, 0, total_rows - 1), owner_start, total_rows)
    slot_index = (
        aggregate_ids(jnp.clip(neighbour, 0, total_rows - 1), owner_start, total_rows)
        - row_aggs[:, None]
        + W
    )
    select = (
        (slot_index[..., None] == jnp.arange(KC, dtype=jnp.int32)) & is_valid[..., None]
    ).astype(jnp.float32)
    applied = jnp.einsum(
        "rkq,rkac->rqac", select, products, precision=lax.Precision.HIGHEST
    ).astype(jnp.bfloat16)
    own_rows = window[W : W + count_rows]
    return jnp.einsum("rbx,rqby->rqxy", own_rows, applied, preferred_element_type=jnp.float32)


def shards(a_blocks, nbr_offset, nbr_count, prolong, owner_start):
    devices_all = lax.axis_size(("dom", "sub"))
    position = lax.axis_index(("dom", "sub"))
    rows_here = a_blocks.shape[0]
    total_rows = devices_all * rows_here
    fine_ids = position * rows_here + jnp.arange(rows_here, dtype=jnp.int32)
    padded = with_halo(prolong, ((("dom", "sub"), 0),), W)
    width_out = KC * prolong.shape[2] * prolong.shape[2]
    own_terms = galerkin_rows(
        a_blocks, padded, nbr_offset, nbr_count, fine_ids, owner_start, total_rows
    )
    local_aggs = aggregate_ids(fine_ids, owner_start, total_rows) - position * AD + AD
    select = (local_aggs[None, :] == jnp.arange(2 * AD, dtype=jnp.int32)[:, None]).astype(
        jnp.float32
    )
    summed = jnp.dot(
        select, own_terms.reshape(rows_here, width_out), precision=lax.Precision.HIGHEST
    )
    summed = summed.reshape(2 * AD, KC, prolong.shape[2], prolong.shape[2])
    received = passed_along(summed[:AD], ("dom", "sub"), -1)
    coarse = summed[AD:] + received
    return coarse


def solution(mesh):
    placed = (
        P(("dom", "sub"), None, None, None),
        P(("dom", "sub"), None),
        P(("dom", "sub")),
        P(("dom", "sub"), None, None),
        P(),
    )
    return jax.shard_map(
        shards,
        mesh=mesh,
        in_specs=placed,
        out_specs=P(("dom", "sub"), None, None, None),
        check_vma=False,
    )
```

profile of v0, /device:TPU:23, one launch (start us, length us, event | category | flops | bytes accessed | tf_op | source)
XLA Modules:
  0.0 355.5 jit_solution(6502806415187356180)
XLA Ops:
  0.0 1.0 fusion.25
  1.0 2.6 collective-permute-start.1
  3.5 4.8 %collective-permute-start = (bf16[3,128,128]{2,1,0:T(8,128)(2,1)S(1)}, bf16[3,128,128]{2,1,0:T(8,128)(2,1)S(1)}, u32[]{:S(2)}, u32[]{:S(2)}) collective-permute-start(bf16[3,128,128]{2,1,0:T(8,128)(2,1)S(1)} %get-tuple-element.65), channel_id=1, source_target_pairs={{0,1},{1,2},{2,3},{3,4},{4,5},{5,6},{6,7},{7,8},{8,9},{9,10},{10,1... | collective-permute-start | bytes 294920 | tf_op jit(solution)/shard_map/ppermute | solution.py:18
  8.3 2.1 fusion.26
  10.4 1.8 fusion.27
  12.3 0.7 add_clamp_fusion
  13.0 0.1 copy.24
  13.1 0.1 reshape.286
  13.2 0.1 copy.17
  13.3 0.1 le.43
  13.4 0.7 convert_reduce_fusion
  14.1 0.1 mul.54
  14.2 0.1 copy.21
  14.3 4.3 %compare_select_fusion.3 = (s32[512,1]{0,1:T(1,128)S(1)}, s32[512,1]{0,1:T(1,128)S(1)}, s32[512,1]{0,1:T(1,128)S(1)}, s32[512,1]{0,1:T(1,128)S(1)}) fusion(s32[]{:T(128)} %bitcast.29, s32[]{:T(128)} %bitcast.30, s32[]{:T(128)} %bitcast.31, s32[]{:T(128)} %bitcast.32, s32[]{:T(128)} %bitcast.33, s32[]{:T(128)} %bitcast.35, s32[]{:T(128)} %bitcast.34, ...), kind=kLoop, calls=%fused_computation.56 | loop fusion | flops 15872 | bytes 10268 | tf_op jit(solution)/shard_map/gather | solution.py:35
  18.6 0.3 compare_reduce_fusion.25
  18.9 15.8 %select_select_fusion.1 = s32[512]{0:T(512)S(1)} fusion(pred[512]{0:T(512)(128)(4,1)S(1)} %get-tuple-element.109, pred[512]{0:T(512)(128)(4,1)S(1)} %get-tuple-element.110, pred[512]{0:T(512)(128)(4,1)S(1)} %get-tuple-element.111, pred[512]{0:T(512)(128)(4,1)S(1)} %get-tuple-element.112, pred[512]{0:T(512)(128)(4,1)S(1)} %get-tuple-element.113, ...), kind=kLoop, calls=%fused_computation.116 | loop fusion | flops 13312 | bytes 17508 | tf_op jit(solution)/shard_map/gather | solution.py:34
  34.7 0.1 gather.28
  34.8 0.1 copy.18
  34.9 15.8 %select_select_fusion = s32[512]{0:T(512)S(1)} fusion(pred[512]{0:T(512)(128)(4,1)S(1)} %get-tuple-element.30, pred[512]{0:T(512)(128)(4,1)S(1)} %get-tuple-element.29, pred[512]{0:T(512)(128)(4,1)S(1)} %get-tuple-element.28, pred[512]{0:T(512)(128)(4,1)S(1)} %get-tuple-element.27, pred[512]{0:T(512)(128)(4,1)S(1)} %get-tuple-element.26, ...), kind=kLoop, calls=%fused_computation.115 | loop fusion | flops 13312 | bytes 17508 | tf_op jit(solution)/shard_map/gather | solution.py:35
  50.7 0.1 gather.30
  50.8 0.1 copy.19
  50.8 0.8 convert_reduce_fusion.2
  51.6 0.7 pad_add_fusion
  52.3 0.8 gather_fusion.3
  53.1 0.8 gather_fusion.2
  53.9 0.8 gather_fusion.1
  54.7 0.8 gather_fusion
  55.5 0.1 multiply_add_fusion
  55.6 0.1 fusion.17
  55.8 0.1 copy.22
  55.8 0.7 fusion.20
  56.5 0.1 copy.23
  56.7 0.0 collective-permute-done.1
  56.7 0.0 collective-permute-done
  56.7 1.9 pad_maximum_fusion
  58.6 14.1 %gather_fusion.4 = bf16[512,128,128]{2,1,0:T(8,128)(2,1)} fusion(bf16[70,128,128]{2,1,0:T(8,128)(2,1)S(1)} %pad_maximum_fusion, s32[1024]{0:T(1024)S(1)} %pad_clamp_fusion), kind=kCustom, calls=%fused_computation.4 | custom fusion | bytes 33556480 | tf_op jit(solution)/shard_map/gather | solution.py:44
  72.6 25.2 %convolution_bitcast_fusion = f32[64,8,128,128]{2,3,1,0:T(8,128)} fusion(bf16[64,8,128,128]{3,2,1,0:T(8,128)(2,1)} %bitcast.91, bf16[64,8,128,128]{3,2,1,0:T(8,128)(2,1)} %param.5), kind=kOutput, calls=%fused_computation.10 | convolution fusion | flops 2147483648 | bytes 67108864 | tf_op jit(solution)/shard_map/rkab,rkbc->rkac/dot_general | solution.py:45
  97.8 33.4 %copy.26 = f32[64,8,128,128]{3,1,2,0:T(8,128)} copy(f32[64,8,128,128]{2,3,1,0:T(8,128)} %convolution_bitcast_fusion) | data formatting | bytes 67108864 | tf_op jit(solution)/shard_map/rkab,rkbc->rkac/dot_general | solution.py:45
  131.2 23.3 %convolution_convert_fusion = bf16[64,7,128,128]{3,1,2,0:T(8,128)(2,1)} fusion(f32[64,8,128,128]{3,1,2,0:T(8,128)} %copy.26, s32[64,8]{1,0:T(8,128)S(1)} %copy.22, pred[64,8]{1,0:T(8,128)(4,1)S(1)} %copy.23), kind=kOutput, calls=%fused_computation.12 | convolution fusion | flops 711990272 | bytes 48237056 | tf_op jit(solution)/shard_map/rkq,rkac->rqac/dot_general | solution.py:61
  154.5 16.0 %fusion.5 = f32[64,7,128,128]{2,3,1,0:T(8,128)} fusion(bf16[64,7,128,128]{3,1,2,0:T(8,128)(2,1)} %convolution_convert_fusion, bf16[64,128,128]{2,1,0:T(8,128)(2,1)S(1)} %copy-done), kind=kOutput, calls=%fused_computation.11 | convolution fusion | flops 1879048192 | bytes 46137344 | tf_op jit(solution)/shard_map/rbx,rqby->rqxy/dot_general | solution.py:65
  170.5 31.0 %copy.28 = f32[64,7,128,128]{3,2,1,0:T(8,128)} copy(f32[64,7,128,128]{2,3,1,0:T(8,128)} %fusion.5) | data formatting | bytes 58720256 | tf_op jit(solution)/shard_map/rbx,rqby->rqxy/transpose | solution.py:65
  201.5 40.9 %fusion = f32[32,114688]{1,0:T(8,128)} fusion(f32[8,8,896,128]{3,2,1,0:T(8,128)} %bitcast.90, s32[64]{0:T(128)S(1)} %get-tuple-element.108), kind=kOutput, calls=%fused_computation.5 | convolution fusion | flops 2818574336 | bytes 44040448 | tf_op jit(solution)/shard_map/dot_general | solution.py:83
  242.4 11.5 %slice_bitcast_fusion = (f32[2,8,896,128]{3,1,2,0:T(8,128)}, f32[2,8,896,128]{3,1,2,0:T(8,128)}) fusion(f32[32,114688]{1,0:T(8,128)} %fusion), kind=kLoop, calls=%fused_computation.13 | loop fusion | bytes 29360128
  253.8 7.6 %copy.34 = f32[2,8,896,128]{3,2,1,0:T(8,128)} copy(f32[2,8,896,128]{3,1,2,0:T(8,128)} %get-tuple-element.63) | data formatting | bytes 14680064
  261.5 2.2 collective-permute-start.2
  263.7 1.4 copy.33
  265.1 82.0 %collective-permute-done.2 = f32[16,7,128,128]{3,2,1,0:T(8,128)} collective-permute-done((f32[16,7,128,128]{3,2,1,0:T(8,128)}, f32[16,7,128,128]{3,2,1,0:T(8,128)}, u32[]{:S(2)}, u32[]{:S(2)}) %collective-permute-start.2) | collective-permute-done | bytes 7340064 | tf_op jit(solution)/shard_map/ppermute | solution.py:27
  347.1 8.4 %add.269 = f32[16,7,128,128]{3,2,1,0:T(8,128)} add(f32[16,7,128,128]{3,2,1,0:T(8,128)S(1)} %bitcast.94, f32[16,7,128,128]{3,2,1,0:T(8,128)} %collective-permute-done.2) | non-fusion elementwise | flops 1835008 | bytes 22020096 | tf_op jit(solution)/shard_map/add | solution.py:88
  (18 shorter events, 0.1 us)
Async XLA Ops:
  1.0 55.7 %collective-permute-start.1 = (bf16[3,128,128]{2,1,0:T(8,128)(2,1)S(1)}, bf16[3,128,128]{2,1,0:T(8,128)(2,1)S(1)}, u32[]{:S(2)}, u32[]{:S(2)}) collective-permute-start(bf16[3,128,128]{2,1,0:T(8,128)(2,1)S(1)} %get-tuple-element.66), channel_id=1, source_target_pairs={{1,0},{2,1},{3,2},{4,3},{5,4},{6,5},{7,6},{8,7},{9,8},{10,9},{11,1... | collective-permute-start | bytes 294920 | tf_op jit(solution)/shard_map/ppermute | solution.py:19
  3.5 53.1 %collective-permute-start = (bf16[3,128,128]{2,1,0:T(8,128)(2,1)S(1)}, bf16[3,128,128]{2,1,0:T(8,128)(2,1)S(1)}, u32[]{:S(2)}, u32[]{:S(2)}) collective-permute-start(bf16[3,128,128]{2,1,0:T(8,128)(2,1)S(1)} %get-tuple-element.65), channel_id=1, source_target_pairs={{0,1},{1,2},{2,3},{3,4},{4,5},{5,6},{6,7},{7,8},{8,9},{9,10},{10,1... | collective-permute-start | bytes 294920 | tf_op jit(solution)/shard_map/ppermute | solution.py:18
  131.2 23.3 %copy-start = (bf16[64,128,128]{2,1,0:T(8,128)(2,1)S(1)}, bf16[64,128,128]{2,1,0:T(8,128)(2,1)}, u32[]{:S(2)}) copy-start(bf16[64,128,128]{2,1,0:T(8,128)(2,1)} %param.8) | copy-start | bytes 6291460
  253.8 9.8 %slice-start = ((s8[7340032]{0:T(1024)(128)(4,1)}), s8[4194304]{0:T(1024)(128)(4,1)S(1)}, s32[]{:S(2)}) async-start(s8[7340032]{0:T(1024)(128)(4,1)} %bitcast.92), calls=%async_computation | async-start | bytes 8388608
  253.8 9.8 %slice-start.1 = ((s8[7340032]{0:T(1024)(128)(4,1)}), s8[3145728]{0:T(1024)(128)(4,1)S(1)}, s32[]{:S(2)}) async-start(s8[7340032]{0:T(1024)(128)(4,1)} %bitcast.92), calls=%async_computation.1 | async-start | bytes 6291456
  261.5 85.6 %collective-permute-start.2 = (f32[16,7,128,128]{3,2,1,0:T(8,128)}, f32[16,7,128,128]{3,2,1,0:T(8,128)}, u32[]{:S(2)}, u32[]{:S(2)}) collective-permute-start(f32[16,7,128,128]{3,2,1,0:T(8,128)} %bitcast.58), channel_id=1, source_target_pairs={{1,0},{2,1},{3,2},{4,3},{5,4},{6,5},{7,6},{8,7},{9,8},{10,9},{11,1... | collective-permute-start | bytes 22020104 | tf_op jit(solution)/shard_map/ppermute | solution.py:27
where the time goes:
time: 358 us; the launch traced here: 356 us
  local copies, waits for them, and re-layouts  108 us (30%)
  matrix products  105 us (29%)
  waiting for transfers between devices  82 us (23%)
  other arithmetic  50.5 us (14%)
  starting transfers between devices  9.53 us (3%)
    ppermute x1, waiting for transfers between devices, passed_along(): return lax.ppermute(block, axis, route)  82 us
    dot_general x1, matrix products, shards(): jnp.dot(select, own_terms.reshape(rows_here, width_out), precision=lax.Pr...  40.9 us
    dot_general x1, local copies, waits for them, and re-layouts, galerkin_rows(): jnp.einsum('rkab,rkbc->rkac', blocks, near_rows, preferred_element_type=j...  33.4 us
    transpose x1, local copies, waits for them, and re-layouts, galerkin_rows(): jnp.einsum('rbx,rqby->rqxy', own_rows, applied, preferred_element_type=jn...  31 us
    dot_general x1, matrix products, galerkin_rows(): jnp.einsum('rkab,rkbc->rkac', blocks, near_rows, preferred_element_type=j...  25.2 us
    dot_general x1, matrix products, galerkin_rows(): jnp.einsum('rkq,rkac->rqac', select, products, precision=lax.Precision.HI...  23.3 us
    unnamed x9, local copies, waits for them, and re-layouts  20.5 us
    gather x5, other arithmetic, aggregate_ids(): span_rows = bounds[owner_index + 1] - first_row  20.5 us
  transfers between devices with their start and end apart: 3, of which 1 were waited for; matrix products, arithmetic and copies ran while one was open for 14% of the time, Pallas kernels for 0%

commit v1 on v0

v1 whole, which is shorter than its diff:
```python
import functools

import jax
import jax.numpy as jnp
from jax import lax
from jax.experimental import pallas as pl
from jax.experimental.pallas import tpu as pltpu
from jax.sharding import PartitionSpec as P

W = 3
KC = 7
AD = 16
SMAX = 48
NQ = 4
UNROLL = 4
HALF = 22
AXES = ("dom", "sub")

T_AGG = 0
T_OFF = 128
T_BASE = 256
T_DST = 384
T_N = 448
T_H = 449
T_LO = 450
T_HI = 451
T_S = 452
T_LEN = 512


def scan_rows(pos, devices, rows, own_ref, table):
    def start(owner):
        inside = (owner >= 0) & (owner < devices)
        at = jnp.clip(owner, 0, devices - 1)
        return jnp.where(inside, own_ref[at], jnp.where(owner < 0, 0, devices * rows))

    total = devices * rows
    first = pos * rows
    begin0, begin1, begin2, begin3 = (start(pos - 1), start(pos), start(pos + 1), start(pos + 2))
    row = jnp.maximum(first - W, 0)
    below = row < begin1
    length = jnp.maximum(jnp.where(below, begin1 - begin0, begin2 - begin1), 1)
    scaled = (row - jnp.where(below, begin0, begin1)) * AD
    local = lax.div(scaled, length)
    agg = jnp.where(below, 0, AD) + local
    rest = scaled - local * length

    def step(at, carry):
        agg, rest = carry
        table[T_AGG + at] = agg
        here = first + at - W
        moves = (here >= 0) & (here < total - 1)
        then = here + 1
        length = jnp.where(
            then >= begin2, begin3 - begin2, jnp.where(then >= begin1, begin2 - begin1, begin1 - begin0)
        )
        more = rest + AD
        wraps = more >= length
        agg_next = jnp.where(wraps, agg + 1, agg)
        rest_next = jnp.where(wraps, more - length, more)
        opens1 = then == begin1
        opens2 = then == begin2
        agg_next = jnp.where(opens1, AD, jnp.where(opens2, 2 * AD, agg_next))
        rest_next = jnp.where(opens1 | opens2, 0, rest_next)
        return jnp.where(moves, agg_next, agg), jnp.where(moves, rest_next, rest)

    lax.fori_loop(0, rows + 2 * W, step, (agg, rest))
    return begin1 - first


def scan_sent(count, table):
    def step(at, carry):
        off, end, begin, floor = carry
        opens = (at == 0) | (table[T_AGG + at + W] != table[T_AGG + jnp.maximum(at - 1, 0) + W])
        off = jnp.where(opens, end - table[T_AGG + at], off)
        begin = jnp.where(opens, end, begin)
        table[T_OFF + at] = off
        table[T_BASE + at] = begin
        end = off + table[T_AGG + at + 2 * W] + 1
        floor = jnp.where((at < W) | (begin < floor), end, floor)
        return off, end, begin, floor

    _, end, _, floor = lax.fori_loop(0, count, step, (0, 0, 0, 0))
    split = jnp.maximum(end - HALF, floor)

    def find(at, carry):
        low, high, begin = carry
        base = table[T_BASE + at]
        fresh = (base <= split) & (base != begin)
        low = jnp.where(fresh, at, low)
        begin = jnp.where(fresh, base, begin)
        high = jnp.where(base < split, at + 1, high)
        return low, high, begin

    low, high, _ = lax.fori_loop(0, count, find, (0, 0, -1))
    low = jnp.where(split >= end, count, low)
    return end, split, low, high


def one_row(row, group, valid, first, total, nbr, cnt, table, blocks, window):
    lowest = table[T_AGG + row] + NQ * group
    right = []
    left = []
    slots = blocks.shape[1]
    for k in range(slots):
        near = row + nbr[row, k]
        used = valid & (k < cnt[row]) & (first + near >= 0) & (first + near < total)
        at = jnp.where(used, table[T_AGG + near + W] - lowest, -1)
        value = window[near + W]
        zero = jnp.zeros_like(value)
        right.append(jnp.concatenate([jnp.where(at == q, value, zero) for q in range(NQ)], axis=1))
        left.append(blocks[row, k])
    applied = jnp.dot(
        jnp.concatenate(left, axis=1), jnp.concatenate(right, axis=0), preferred_element_type=jnp.float32
    ).astype(jnp.bfloat16)
    return lax.dot_general(
        window[row + W], applied, (((0,), (0,)), ((), ())), preferred_element_type=jnp.float32
    )


def all_rows(lo, hi, low_slot, high_slot, own, first, total, nbr, cnt, table, blocks, window, row_sems, a_hbm, acc):
    trash = acc.shape[0] - 1
    width = window.shape[2]

    def add(row, group, valid, term):
        agg = table[T_AGG + row + W]
        highest = table[T_AGG + row + 2 * W]
        off = (KC - 1) * agg - KC * AD + W if own else table[T_OFF + row]
        for q in range(NQ):
            target = table[T_AGG + row] + NQ * group + q
            slot = off + target
            ok = valid & (target <= highest) & (slot >= low_slot) & (slot < high_slot)
            at = jnp.where(ok, slot - low_slot, trash)
            acc[at] += term[:, q * width : (q + 1) * width]

    def block(step, carry):
        begin = lo + step * UNROLL
        for u in range(UNROLL):

            @pl.when(begin + u < hi)
            def _():
                row = begin + u
                pltpu.make_async_copy(a_hbm.at[row], blocks.at[row], row_sems.at[row]).wait()

        terms = []
        for u in range(UNROLL):
            valid = begin + u < hi
            row = jnp.minimum(begin + u, hi - 1)
            terms.append((row, valid, one_row(row, 0, valid, first, total, nbr, cnt, table, blocks, window)))
        for row, valid, term in terms:
            add(row, 0, valid, term)
        return carry

    lax.fori_loop(0, lax.div(hi - lo + UNROLL - 1, UNROLL), block, 0)

    def wide(row, carry):
        @pl.when(table[T_AGG + row + 2 * W] - table[T_AGG + row] >= NQ)
        def _():
            term = one_row(row, 1, True, first, total, nbr, cnt, table, blocks, window)
            add(row, 1, True, term)

        return carry

    lax.fori_loop(lo, hi, wide, 0)


def start_rows(lo, hi, a_hbm, blocks, row_sems):
    def step(row, carry):
        pltpu.make_async_copy(a_hbm.at[row], blocks.at[row], row_sems.at[row]).start()
        return carry

    lax.fori_loop(lo, hi, step, 0)


def clear(acc, count):
    def step(at, carry):
        acc[at] = jnp.zeros(acc.shape[1:], acc.dtype)
        return carry

    lax.fori_loop(0, count, step, 0)


def late_kernel(devices, pos_ref, own_ref, nbr, cnt, a_hbm, p_hbm, out, table, blocks, window, acc, sem, row_sems):
    rows = a_hbm.shape[0]
    pos = pos_ref[0]
    copy = pltpu.make_async_copy(p_hbm, window.at[pl.ds(W, rows)], sem)
    copy.start()
    count = scan_rows(pos, devices, rows, own_ref, table)
    end, split, low, high = scan_sent(count, table)
    start_rows(low, count, a_hbm, blocks, row_sems)
    table[T_N] = end
    table[T_H] = split
    table[T_LO] = low
    table[T_HI] = high
    table[T_S] = count
    clear(acc, HALF)
    copy.wait()
    all_rows(
        low, count, split, end, False, pos * rows, devices * rows, nbr, cnt, table, blocks, window, row_sems, a_hbm, acc
    )

    def give(at, carry):
        out[at] = acc[at].astype(out.dtype)
        return carry

    lax.fori_loop(0, HALF, give, 0)


def early_kernel(
    devices, pos_ref, own_ref, nbr, cnt, table, a_hbm, p_hbm, before, out, merge, blocks, window, acc, sem, sem2, row_sems
):
    rows = a_hbm.shape[0]
    pos = pos_ref[0]
    high = table[T_HI]
    copy = pltpu.make_async_copy(p_hbm, window.at[pl.ds(W, rows)], sem)
    copy.start()
    edge = pltpu.make_async_copy(before, window.at[pl.ds(0, W)], sem2)
    edge.start()
    start_rows(0, high, a_hbm, blocks, row_sems)
    clear(acc, HALF)
    copy.wait()
    edge.wait()
    all_rows(
        0, high, 0, table[T_H], False, pos * rows, devices * rows, nbr, cnt, table, blocks, window, row_sems, a_hbm, acc
    )

    def give(at, carry):
        out[at] = acc[at].astype(out.dtype)
        return carry

    lax.fori_loop(0, HALF, give, 0)

    count = jnp.where(
        pos + 1 < devices, scan_rows(pos + 1, devices, rows, own_ref, merge), 0
    )
    end, split, _, _ = scan_sent(count, merge)

    def place(row, done):
        agg = merge[T_AGG + row + W]

        def put(slot, carry):
            merge[T_DST + slot] = (KC - 1) * agg + W + slot - merge[T_OFF + row]
            return carry

        last = merge[T_OFF + row] + merge[T_AGG + row + 2 * W] + 1
        lax.fori_loop(done, last, put, 0)
        return last

    lax.fori_loop(0, count, place, 0)
    merge[T_N] = end
    merge[T_H] = split


def own_kernel(
    devices, pos_ref, nbr, cnt, table, order, a_hbm, p_hbm, before, after, out, blocks, window, acc, sem, sem2, sem3, sem4, row_sems
):
    rows = a_hbm.shape[0]
    pos = pos_ref[0]
    count = table[T_S]
    copy = pltpu.make_async_copy(p_hbm, window.at[pl.ds(W, rows)], sem)
    copy.start()
    edge = pltpu.make_async_copy(before, window.at[pl.ds(0, W)], sem2)
    edge.start()
    edge2 = pltpu.make_async_copy(after, window.at[pl.ds(W + rows, W)], sem3)
    edge2.start()
    start_rows(count, rows, a_hbm, blocks, row_sems)
    clear(acc, AD * KC)
    copy.wait()
    edge.wait()
    edge2.wait()
    all_rows(
        count, rows, 0, AD * KC, True, pos * rows, devices * rows, nbr, cnt, table, blocks, window, row_sems, a_hbm, acc
    )
    done = pltpu.make_async_copy(acc.at[pl.ds(0, AD * KC)], out, sem4)
    done.start()
    done.wait()


def merge_kernel(upper, merge, got, coarse, out, held, in_sems, out_sems):
    split = merge[T_H]
    begin = split if upper else 0
    count = merge[T_N] - split if upper else split

    def fetch(at):
        return pltpu.make_async_copy(coarse.at[merge[T_DST + begin + at]], held.at[at], in_sems.at[at])

    def store(at):
        return pltpu.make_async_copy(held.at[at], out.at[merge[T_DST + begin + at]], out_sems.at[at])

    def first(at, carry):
        fetch(at).start()
        return carry

    def second(at, carry):
        fetch(at).wait()
        held[at] += got[at].astype(jnp.float32)
        store(at).start()
        return carry

    def third(at, carry):
        store(at).wait()
        return carry

    lax.fori_loop(0, count, first, 0)
    lax.fori_loop(0, count, second, 0)
    lax.fori_loop(0, count, third, 0)


SMEM = pl.BlockSpec(memory_space=pltpu.SMEM)
VMEM = pl.BlockSpec(memory_space=pltpu.VMEM)
ANY = pl.BlockSpec(memory_space=pl.ANY)
DMA = pltpu.SemaphoreType.DMA


def params():
    return pltpu.CompilerParams(vmem_limit_bytes=50 * 1024 * 1024)


def cost(flops, moved):
    return pl.CostEstimate(flops=flops, bytes_accessed=moved, transcendentals=0)


def passed(block, step):
    devices = range(lax.axis_size(AXES))
    return lax.ppermute(block, AXES, [(i, i + step) for i in devices if i + step in devices])


def shards(a_blocks, nbr_offset, nbr_count, prolong, owner_start):
    devices = lax.axis_size(AXES)
    rows, slots, size, width = a_blocks.shape
    pos = lax.axis_index(AXES).reshape(1)
    flops = rows * slots * size * size * width * 2
    moved = rows * slots * size * width * 2
    work = [
        pltpu.VMEM((rows, slots, size, size), jnp.bfloat16),
        pltpu.VMEM((rows + 2 * W, size, width), jnp.bfloat16),
    ]
    table_shape = jax.ShapeDtypeStruct((T_LEN,), jnp.int32)
    sent_shape = jax.ShapeDtypeStruct((HALF, width, width), jnp.bfloat16)

    before = passed(prolong[rows - W :], 1)
    after = passed(prolong[:W], -1)
    late, table = pl.pallas_call(
        functools.partial(late_kernel, devices),
        out_shape=(sent_shape, table_shape),
        in_specs=[SMEM, SMEM, SMEM, SMEM, ANY, ANY],
        out_specs=(VMEM, SMEM),
        scratch_shapes=work
        + [pltpu.VMEM((HALF + 1, width, width), jnp.float32), DMA, DMA((rows,))],
        compiler_params=params(),
        cost_estimate=cost(flops // 2, moved // 2),
        name="late_rows",
    )(pos, owner_start, nbr_offset, nbr_count, a_blocks, prolong)
    got_late = passed(late, -1)
    early, merge = pl.pallas_call(
        functools.partial(early_kernel, devices),
        out_shape=(sent_shape, table_shape),
        in_specs=[SMEM, SMEM, SMEM, SMEM, SMEM, ANY, ANY, ANY],
        out_specs=(VMEM, SMEM),
        scratch_shapes=work
        + [pltpu.VMEM((HALF + 1, width, width), jnp.float32), DMA, DMA, DMA((rows,))],
        compiler_params=params(),
        cost_estimate=cost(flops // 2, moved // 2),
        name="early_rows",
    )(pos, owner_start, nbr_offset, nbr_count, table, a_blocks, prolong, before)
    got_early = passed(early, -1)
    coarse = pl.pallas_call(
        functools.partial(own_kernel, devices),
        out_shape=jax.ShapeDtypeStruct((AD * KC, width, width), jnp.float32),
        in_specs=[SMEM, SMEM, SMEM, SMEM, SMEM, ANY, ANY, ANY, ANY],
        out_specs=ANY,
        scratch_shapes=work
        + [pltpu.VMEM((AD * KC + 1, width, width), jnp.float32), DMA, DMA, DMA, DMA, DMA((rows,))],
        compiler_params=params(),
        cost_estimate=cost(flops, moved),
        name="own_rows",
    )(pos, nbr_offset, nbr_count, table, merge, a_blocks, prolong, before, after)
    for upper, got in ((True, got_late), (False, got_early)):
        coarse = pl.pallas_call(
            functools.partial(merge_kernel, upper),
            out_shape=jax.ShapeDtypeStruct(coarse.shape, coarse.dtype),
            in_specs=[SMEM, VMEM, ANY],
            out_specs=ANY,
            scratch_shapes=[
                pltpu.VMEM((HALF, width, width), jnp.float32),
                DMA((HALF,)),
                DMA((HALF,)),
            ],
            input_output_aliases={2: 0},
            compiler_params=params(),
            name="merge_late" if upper else "merge_early",
        )(merge, got, coarse)
    return coarse.reshape(AD, KC, width, width)


def solution(mesh):
    placed = (
        P(("dom", "sub"), None, None, None),
        P(("dom", "sub"), None),
        P(("dom", "sub")),
        P(("dom", "sub"), None, None),
        P(),
    )
    return jax.shard_map(
        shards,
        mesh=mesh,
        in_specs=placed,
        out_specs=P(("dom", "sub"), None, None, None),
        check_vma=False,
    )
```

time: 358 us -> 87.4 us (0.24)
  the two profiles are of different devices: /device:TPU:23 before, /device:TPU:2 now
where the time goes in v1:
time: 87.4 us
  Pallas kernels  49.5 us (57%)
  starting transfers between devices  25.3 us (29%)
  waiting for transfers between devices  7.92 us (9%)
  local copies, waits for them, and re-layouts  4.63 us (5%)
    pallas_call x1, Pallas kernels, shards(): pl.pallas_call(functools.partial(own_kernel, devices), out_shape=jax.Shap...  28.8 us
    ppermute x4, starting transfers between devices, passed(): lax.ppermute(block, AXES, [(i, i + step) for i in devices if i + step in...  25.3 us
    pallas_call x1, Pallas kernels, shards(): pl.pallas_call(functools.partial(early_kernel, devices), out_shape=(sent_...  8.88 us
    ppermute x4, waiting for transfers between devices, passed(): lax.ppermute(block, AXES, [(i, i + step) for i in devices if i + step in...  7.92 us
    pallas_call x1, Pallas kernels, shards(): pl.pallas_call(functools.partial(late_kernel, devices), out_shape=(sent_s...  6.48 us
    pallas_call x2, Pallas kernels, shards(): pl.pallas_call(functools.partial(merge_kernel, upper), out_shape=jax.Shap...  5.35 us
    unnamed x9, local copies, waits for them, and re-layouts  3.68 us
  transfers between devices with their start and end apart: 4, of which 1 were waited for; matrix products, arithmetic and copies ran while one was open for 1% of the time, Pallas kernels for 54%

profile of v1, /device:TPU:2, one launch (start us, length us, event | category | flops | bytes accessed | tf_op | source)
XLA Modules:
  0.0 87.4 jit_solution(17540398528597996603)
XLA Ops:
  0.0 1.0 %fusion = (bf16[3,128,128]{2,1,0:T(8,128)(2,1)S(1)}, bf16[3,128,128]{2,1,0:T(8,128)(2,1)S(1)}) fusion(bf16[64,128,128]{2,1,0:T(8,128)(2,1)} %p_hbm.5), kind=kLoop, calls=%fused_computation | loop fusion | bytes 393216 | tf_op jit(solution)/shard_map/slice | solution.py:342
  1.0 1.9 %collective-permute-start = (bf16[3,128,128]{2,1,0:T(8,128)(2,1)S(1)}, bf16[3,128,128]{2,1,0:T(8,128)(2,1)S(1)}, u32[]{:S(2)}, u32[]{:S(2)}) collective-permute-start(bf16[3,128,128]{2,1,0:T(8,128)(2,1)S(1)} %get-tuple-element.14), channel_id=1, source_target_pairs={{0,1},{1,2},{2,3},{3,4},{4,5},{5,6},{6,7},{7,8},{8,9},{9,10},{10,1... | collective-permute-start | bytes 294920 | tf_op jit(solution)/shard_map/ppermute | solution.py:325
  2.9 0.8 copy.9.nbr
  3.7 0.0 copy-start
  3.7 1.6 %copy-done = bf16[64,128,128]{2,1,0:T(8,128)(2,1)S(1)} copy-done((bf16[64,128,128]{2,1,0:T(8,128)(2,1)S(1)}, bf16[64,128,128]{2,1,0:T(8,128)(2,1)}, u32[]{:S(2)}) %copy-start) | copy-done | bytes 2097176
  5.3 0.0 copy-start.2
  5.3 0.7 copy-done.2
  5.9 0.0 copy-start.3
  5.9 0.7 copy-done.3
  6.6 6.5 %late_rows.1 = (bf16[22,128,128]{2,1,0:T(8,128)(2,1)S(1)}, s32[512]{0:T(512)S(1)}) custom-call(s32[1]{0:T(128)} %bitcast.pos_ref, s32[32]{0:T(128)S(1)} %copy-done.3, s32[64,8]{1,0:T(8,128)S(1)} %copy.9.nbr, s32[64]{0:T(128)S(1)} %copy-done.2, bf16[64,8,128,128]{3,2,1,0:T(8,128)(2,1)} %a_hbm.5, bf16[64,128,128]{2,1,0:T(8,128)(2,1)S(1)} %copy-done), custom_call_target="tpu_custom_call" | custom-call | flops 1073741824 | bytes 8388608 | tf_op jit(solution)/shard_map/late_rows/pallas_call | solution.py:343
  13.1 19.5 %collective-permute-start.2 = (bf16[22,128,128]{2,1,0:T(8,128)(2,1)S(1)}, bf16[22,128,128]{2,1,0:T(8,128)(2,1)S(1)}, u32[]{:S(2)}, u32[]{:S(2)}) collective-permute-start(bf16[22,128,128]{2,1,0:T(8,128)(2,1)S(1)} %get-tuple-element.12), channel_id=1, source_target_pairs={{1,0},{2,1},{3,2},{4,3},{5,4},{6,5},{7,6},{8,7},{9,8},{10,9},{11,1... | collective-permute-start | bytes 2162696 | tf_op jit(solution)/shard_map/ppermute | solution.py:325
  32.6 0.0 collective-permute-done.before
  32.6 0.0 copy-start.1
  32.6 8.9 %early_rows.1 = (bf16[22,128,128]{2,1,0:T(8,128)(2,1)S(1)}, s32[512]{0:T(512)S(1)}) custom-call(s32[1]{0:T(128)} %bitcast.pos_ref, s32[32]{0:T(128)S(1)} %copy-done.3, s32[64,8]{1,0:T(8,128)S(1)} %copy.9.nbr, s32[64]{0:T(128)S(1)} %copy-done.2, s32[512]{0:T(512)S(1)} %get-tuple-element.9.table, bf16[64,8,128,128]{3,2,1,0:T(8,128)(2,1)} %a_hbm.5, ...), custom_call_target="tpu_custom_call" | custom-call | flops 1073741824 | bytes 8388608 | tf_op jit(solution)/shard_map/early_rows/pallas_call | solution.py:355
  41.5 1.9 %collective-permute-start.1 = (bf16[22,128,128]{2,1,0:T(8,128)(2,1)S(1)}, bf16[22,128,128]{2,1,0:T(8,128)(2,1)S(1)}, u32[]{:S(2)}, u32[]{:S(2)}) collective-permute-start(bf16[22,128,128]{2,1,0:T(8,128)(2,1)S(1)} %get-tuple-element.11), channel_id=1, source_target_pairs={{1,0},{2,1},{3,2},{4,3},{5,4},{6,5},{7,6},{8,7},{9,8},{10,9},{11,1... | collective-permute-start | bytes 2162696 | tf_op jit(solution)/shard_map/ppermute | solution.py:325
  43.4 1.9 %collective-permute-start.3 = (bf16[3,128,128]{2,1,0:T(8,128)(2,1)S(1)}, bf16[3,128,128]{2,1,0:T(8,128)(2,1)S(1)}, u32[]{:S(2)}, u32[]{:S(2)}) collective-permute-start(bf16[3,128,128]{2,1,0:T(8,128)(2,1)S(1)} %get-tuple-element.13), channel_id=1, source_target_pairs={{1,0},{2,1},{3,2},{4,3},{5,4},{6,5},{7,6},{8,7},{9,8},{10,9},{11,1... | collective-permute-start | bytes 294920 | tf_op jit(solution)/shard_map/ppermute | solution.py:325
  45.4 7.9 %collective-permute-done.3.after = bf16[3,128,128]{2,1,0:T(8,128)(2,1)S(1)} collective-permute-done((bf16[3,128,128]{2,1,0:T(8,128)(2,1)S(1)}, bf16[3,128,128]{2,1,0:T(8,128)(2,1)S(1)}, u32[]{:S(2)}, u32[]{:S(2)}) %collective-permute-start.3) | collective-permute-done | bytes 98336 | tf_op jit(solution)/shard_map/ppermute | solution.py:325
  53.3 0.0 copy-done.1
  53.3 28.8 %own_rows.1.coarse = f32[112,128,128]{2,1,0:T(8,128)} custom-call(s32[1]{0:T(128)} %bitcast.pos_ref, s32[64,8]{1,0:T(8,128)S(1)} %copy.9.nbr, s32[64]{0:T(128)S(1)} %copy-done.2, s32[512]{0:T(512)S(1)} %get-tuple-element.9.table, s32[512]{0:T(512)S(1)} %get-tuple-element.10.order.merge, bf16[64,8,128,128]{3,2,1,0:T(8,128)(2,1)} %a_hbm.5, ...), custom_call_target="tpu_custom_call" | custom-call | flops 2147483648 | bytes 16777216 | tf_op jit(solution)/shard_map/own_rows/pallas_call | solution.py:367
  82.1 0.0 collective-permute-done.2.got
  82.1 2.8 %merge_late.1.coarse = f32[112,128,128]{2,1,0:T(8,128)} custom-call(s32[512]{0:T(512)S(1)} %get-tuple-element.10.order.merge, bf16[22,128,128]{2,1,0:T(8,128)(2,1)S(1)} %collective-permute-done.2.got, f32[112,128,128]{2,1,0:T(8,128)} %own_rows.1.coarse), custom_call_target="tpu_custom_call", output_to_operand_aliasing={{}: (2, {})} | custom-call | tf_op jit(solution)/shard_map/merge_late/pallas_call | solution.py:379
  84.9 0.0 collective-permute-done.1.got
  84.9 2.5 %merge_early.1 = f32[112,128,128]{2,1,0:T(8,128)} custom-call(s32[512]{0:T(512)S(1)} %get-tuple-element.10.order.merge, bf16[22,128,128]{2,1,0:T(8,128)(2,1)S(1)} %collective-permute-done.1.got, f32[112,128,128]{2,1,0:T(8,128)} %merge_late.1.coarse), custom_call_target="tpu_custom_call", output_to_operand_aliasing={{}: (2, {})} | custom-call | tf_op jit(solution)/shard_map/merge_early/pallas_call | solution.py:379
Async XLA Ops:
  1.0 31.6 %collective-permute-start = (bf16[3,128,128]{2,1,0:T(8,128)(2,1)S(1)}, bf16[3,128,128]{2,1,0:T(8,128)(2,1)S(1)}, u32[]{:S(2)}, u32[]{:S(2)}) collective-permute-start(bf16[3,128,128]{2,1,0:T(8,128)(2,1)S(1)} %get-tuple-element.14), channel_id=1, source_target_pairs={{0,1},{1,2},{2,3},{3,4},{4,5},{5,6},{6,7},{7,8},{8,9},{9,10},{10,1... | collective-permute-start | bytes 294920 | tf_op jit(solution)/shard_map/ppermute | solution.py:325
  3.7 1.6 %copy-start = (bf16[64,128,128]{2,1,0:T(8,128)(2,1)S(1)}, bf16[64,128,128]{2,1,0:T(8,128)(2,1)}, u32[]{:S(2)}) copy-start(bf16[64,128,128]{2,1,0:T(8,128)(2,1)} %p_hbm.5) | copy-start | bytes 6291460
  5.3 0.7 copy-start.2
  5.9 0.7 copy-start.3
  13.1 69.0 %collective-permute-start.2 = (bf16[22,128,128]{2,1,0:T(8,128)(2,1)S(1)}, bf16[22,128,128]{2,1,0:T(8,128)(2,1)S(1)}, u32[]{:S(2)}, u32[]{:S(2)}) collective-permute-start(bf16[22,128,128]{2,1,0:T(8,128)(2,1)S(1)} %get-tuple-element.12), channel_id=1, source_target_pairs={{1,0},{2,1},{3,2},{4,3},{5,4},{6,5},{7,6},{8,7},{9,8},{10,9},{11,1... | collective-permute-start | bytes 2162696 | tf_op jit(solution)/shard_map/ppermute | solution.py:325
  32.6 20.7 %copy-start.1 = (bf16[64,128,128]{2,1,0:T(8,128)(2,1)S(1)}, bf16[64,128,128]{2,1,0:T(8,128)(2,1)}, u32[]{:S(2)}) copy-start(bf16[64,128,128]{2,1,0:T(8,128)(2,1)} %p_hbm.5) | copy-start | bytes 6291460
  41.5 43.4 %collective-permute-start.1 = (bf16[22,128,128]{2,1,0:T(8,128)(2,1)S(1)}, bf16[22,128,128]{2,1,0:T(8,128)(2,1)S(1)}, u32[]{:S(2)}, u32[]{:S(2)}) collective-permute-start(bf16[22,128,128]{2,1,0:T(8,128)(2,1)S(1)} %get-tuple-element.11), channel_id=1, source_target_pairs={{1,0},{2,1},{3,2},{4,3},{5,4},{6,5},{7,6},{8,7},{9,8},{10,9},{11,1... | collective-permute-start | bytes 2162696 | tf_op jit(solution)/shard_map/ppermute | solution.py:325
  43.4 9.8 %collective-permute-start.3 = (bf16[3,128,128]{2,1,0:T(8,128)(2,1)S(1)}, bf16[3,128,128]{2,1,0:T(8,128)(2,1)S(1)}, u32[]{:S(2)}, u32[]{:S(2)}) collective-permute-start(bf16[3,128,128]{2,1,0:T(8,128)(2,1)S(1)} %get-tuple-element.13), channel_id=1, source_target_pairs={{1,0},{2,1},{3,2},{4,3},{5,4},{6,5},{7,6},{8,7},{9,8},{10,9},{11,1... | collective-permute-start | bytes 294920 | tf_op jit(solution)/shard_map/ppermute | solution.py:325
